TPU v7x, 32 devices: a whole 2x2x4 slice. The times are simulated.
32 devices in a mesh: replica: 4 (over y, x), shard: 8 (over z, core).
Axes of the slice: x: 2, y: 2, z: 4, core: 2. Of those that a mesh axis runs over, the one named last changes fastest.
Arguments:
- images: float32 [96, 7, 7, 512], P(('replica', 'shard')), may hold values from -6 to 6
- filters: float32 [1, 512, 4608], P(None, 'shard'), may hold values from -0.09375 to 0.09375
- out_grad: float32 [96, 7, 7, 512], P(('replica', 'shard')), may hold values from -6 to 6
Outputs:
- conv_out: float32 [96, 7, 7, 512], P(('replica', 'shard'))
- filter_grad: float32 [1, 512, 4608], P(None, 'shard', 'replica')
All inputs are finite; a program needn't handle non-finite values.
Results may differ from a plain program's by a relative error of at most 0.0003.
Values sent between devices are 32-bit elements; how exact they have to be, the bound alone decides.
No kernel may reach another device: no remote copies, remote signals or barrier semaphores. Data moves between devices by JAX's collectives and lax.ppermute only.
A program may use at most 256 MiB of HBM per device.

v0:
```python
import functools

import jax
import jax.numpy as jnp
from jax import lax
from jax.experimental import pallas as pl
from jax.experimental.pallas import tpu as pltpu
from jax.sharding import PartitionSpec as P

CORES = 2
LANES = 128
LINE = 8
CHUNK_SHARES = (2, 2)
VMEM = pl.BlockSpec(memory_space=pltpu.VMEM)
SMEM = pl.BlockSpec(memory_space=pltpu.SMEM)


def call(kernel, name, out_shape, operands, scratch=(), mib=24):
    return pl.pallas_call(
        kernel,
        out_shape=out_shape,
        in_specs=[SMEM] + [VMEM] * (len(operands) - 1),
        out_specs=[VMEM] * len(out_shape),
        scratch_shapes=list(scratch),
        compiler_params=pltpu.CompilerParams(vmem_limit_bytes=mib * 1024 * 1024),
        cost_estimate=pl.CostEstimate(flops=0, bytes_accessed=0, transcendentals=0),
        name=name,
    )(*operands)


def chunk_units(width):
    units = width // LANES
    share = units // sum(CHUNK_SHARES)
    bounds = [0]
    for part in CHUNK_SHARES:
        bounds.append(bounds[-1] + part * share)
    bounds[-1] = units
    return [list(range(a, b)) for a, b in zip(bounds, bounds[1:])]


def exchange_plan(width, replicas):
    units = width // LANES
    span = 9 * units // replicas
    chunks = chunk_units(width)
    late = [[] for _ in range(replicas)]
    plan = []
    for index, chunk in enumerate(chunks):
        mine = [
            [(t, u) for t in range(9) for u in chunk if (t * units + u) // span == q]
            for q in range(replicas)
        ]
        if index + 1 < len(chunks):
            base = min(len(m) for m in mine)
            for q in range(replicas):
                late[q] += mine[q][base:]
                mine[q] = mine[q][:base]
        else:
            mine = [m + extra for m, extra in zip(mine, late)]
        plan.append(mine)
    return plan


def partner(rep, step, count):
    return (rep + step) % count if count & (count - 1) else rep ^ step


def slot_of(owner, rep, count):
    if count & (count - 1):
        return lax.rem(owner - rep + count, count)
    return jnp.bitwise_xor(jnp.int32(owner), rep)


def after(value, *others):
    return lax.optimization_barrier((value, *others))[0]


def split(value):
    high = value.astype(jnp.bfloat16).astype(jnp.float32)
    return high, value - high


def deep_rows(first, second, third):
    rows, lanes = first.shape
    full = rows // LANES * LANES
    pieces = [p[:full] for p in (first, second, third)] if full else []
    rest = 3 * (rows - full)
    if rest:
        pieces += [p[full:] for p in (first, second, third)]
        gap = -rest % LANES
        if gap:
            pieces.append(jnp.zeros((gap, lanes), jnp.float32))
    return jnp.concatenate(pieces, axis=0)


def dot_nt(lhs, rhs):
    return lax.dot_general(
        lhs, rhs, (((1,), (1,)), ((), ())), preferred_element_type=jnp.float32
    )


def dot_nn(lhs, rhs):
    return lax.dot_general(
        lhs, rhs, (((1,), (0,)), ((), ())), preferred_element_type=jnp.float32
    )


def pack_kernel(chunks, parts, ids, image_ref, grad_ref, *refs):
    up_ref, down_ref, *chunk_refs, own_ref = refs
    count, rows, cols, width = image_ref.shape
    dense = count * rows * cols
    spare = own_ref.shape[1] - dense

    def pack(src, lanes, targets):
        for b in range(count):
            for h in range(rows):
                at = (b * rows + h) * cols
                value = src[b, h, :, lanes]
                for ref, p in targets:
                    ref[p, at : at + cols, :] = value
        if spare:
            for ref, p in targets:
                ref[p, dense:, :] = jnp.zeros((spare, LANES), jnp.float32)

    for p, unit in enumerate(chunks[0]):
        pack(image_ref, pl.ds(unit * LANES, LANES), [(up_ref, p), (down_ref, p)])
    for ref, units in zip(chunk_refs, chunks[1:]):
        for p, unit in enumerate(units):
            pack(image_ref, pl.ds(unit * LANES, LANES), [(ref, p)])
    for d in range(parts):
        start = ids[2 + d] * LANES
        if d == 0:
            target = (own_ref, 0)
        elif d <= parts // 2:
            target = (up_ref, up_ref.shape[0] - d)
        else:
            target = (down_ref, down_ref.shape[0] - (parts - d))
        pack(grad_ref, pl.ds(pl.multiple_of(start, LANES), LANES), [target])


def join_kernel(parts, ids, *refs):
    out_ref = refs[-1]
    count, rows, cols, width = out_ref.shape
    for d in range(parts):
        start = ids[2 + (parts - d) % parts] * LANES
        lanes = pl.ds(pl.multiple_of(start, LANES), LANES)
        for b in range(count):
            for h in range(rows):
                at = (b * rows + h) * cols
                out_ref[b, h, :, lanes] = refs[d][at : at + cols, :]


def filter_kernel(chunks, ids, own_ref, mate_ref, *out_refs):
    owned, kdim = own_ref.shape[1:]
    width = kdim // 9
    first = ids[0] == 0
    for tap in range(9):
        rows = slice(tap * 2 * owned, (tap + 1) * 2 * owned)
        for ref, units in zip(out_refs, chunks):
            size = len(units) * LANES
            at = tap * width + units[0] * LANES
            own = own_ref[0, :, at : at + size]
            mate = mate_ref[0, :, at : at + size]
            both = jnp.concatenate(
                [jnp.where(first, own, mate), jnp.where(first, mate, own)], axis=0
            )
            high, low = split(both)
            high = high.astype(jnp.bfloat16)
            ref[rows, :size] = high
            ref[rows, size : 2 * size] = high
            ref[rows, 2 * size :] = low.astype(jnp.bfloat16)


def grad_kernel(shape, ids, *refs):
    count, rows, cols = shape
    *refs, pad_ref = refs
    in_refs, out_refs = refs[: len(refs) // 2], refs[len(refs) // 2 :]
    block = (rows + 2) * LINE
    pad_ref[...] = jnp.zeros_like(pad_ref)
    for in_ref, out_ref in zip(in_refs, out_refs):
        piece = in_ref.shape[0] - 1
        for b in range(count):
            for h in range(rows):
                at = LINE + b * block + (h + 1) * LINE
                dense = (b * rows + h) * cols
                pad_ref[at : at + cols, :] = in_ref[piece, dense : dense + cols, :]
        for tap in range(9):
            a, c = tap // 3, tap % 3
            pieces = []
            for b in range(count):
                start = LINE + b * block + (2 - a) * LINE - (c - 1)
                pieces.append(pad_ref[start : start + rows * LINE, :])
            high, low = split(jnp.concatenate(pieces, axis=0))
            deep = deep_rows(high, high, low)
            out_ref[tap * LANES : (tap + 1) * LANES, :] = jnp.transpose(deep).astype(
                jnp.bfloat16
            )


def tap_products(shape, chunks, blocks, high, low, w_refs, conv_refs, y_ref):
    count, height, cols = shape
    block = height * LINE
    real = count * block
    high, low = high.astype(jnp.bfloat16), low.astype(jnp.bfloat16)
    for start in range(0, 9 * LANES, 2 * LANES):
        out = slice(start, min(start + 2 * LANES, 9 * LANES))
        lane, product = 0, None
        for ref, chunk in zip(w_refs, chunks):
            lanes = slice(lane, lane + len(chunk) * LANES)
            packed = jnp.concatenate([high[:, lanes], low[:, lanes], high[:, lanes]], axis=1)
            part = dot_nt(packed, ref[out, :])
            product = part if product is None else product + part
            lane += len(chunk) * LANES
        y_ref[:, out] = product
    gap = jnp.zeros((LINE, LANES), jnp.float32)
    for j, conv_ref in enumerate(conv_refs):
        for b in range(count):
            at = j * real + b * block
            sums = []
            for c in range(3):
                above, middle, below = (
                    y_ref[at : at + block, (3 * a + c) * LANES : (3 * a + c + 1) * LANES]
                    for a in range(3)
                )
                sums.append(
                    middle
                    + jnp.concatenate([gap, above[:-LINE]], axis=0)
                    + jnp.concatenate([below[LINE:], gap], axis=0)
                )
            result = (
                sums[1]
                + pltpu.roll(sums[0], 1, axis=0)
                + pltpu.roll(sums[2], block - 1, axis=0)
            )
            for h in range(height):
                dense = (b * height + h) * cols
                conv_ref[dense : dense + cols, :] = result[h * LINE : h * LINE + cols]
        spare = conv_ref.shape[0] - count * height * cols
        if spare:
            conv_ref[count * height * cols :, :] = jnp.zeros((spare, LANES), jnp.float32)


def multiply_kernel(shape, chunks, summed, plan, late, blocks, begun, done, convolve, ids, *refs):
    refs = list(refs)

    def take(k):
        return [refs.pop(0) for _ in range(k)]

    x_refs, g_refs = [take(len(chunks)) for _ in range(blocks)], take(blocks)
    w_refs = take(len(chunks)) if convolve else []
    sum_ref = take(1)[0] if begun is not None else None
    extra_refs = take(len(late)) if done and convolve else []
    conv_refs = take(blocks) if convolve else []
    if done:
        own_ref, mate_ref = take(2)
        extra_out = take(1)[0] if late and not convolve else None
    else:
        (total_ref,) = take(1)
    rows_ref, *y_ref = refs
    count, height, cols = shape
    block = height * LINE
    real = count * block
    first = ids[0] == 0

    rows_ref[...] = jnp.zeros_like(rows_ref)
    for j in range(blocks):
        lane = 0
        for ref, chunk in zip(x_refs[j], chunks):
            for p in range(len(chunk)):
                for line in range(count * height):
                    at = j * real + line * LINE
                    rows_ref[at : at + cols, lane : lane + LANES] = ref[
                        p, line * cols : (line + 1) * cols, :
                    ]
                lane += LANES
    high, low = split(rows_ref[...])

    if convolve:
        tap_products(shape, chunks, blocks, high, low, w_refs, conv_refs, *y_ref)

    places = {pair: (q, i) for q, pairs in enumerate(plan) for i, pair in enumerate(pairs)}
    skip = sum(len(c) for c in chunks if c[0] < summed[0]) * LANES
    lanes = slice(skip, skip + len(summed) * LANES)
    deeps = [
        deep_rows(*(v[j * real : (j + 1) * real, lanes] for v in (high, low, high))).astype(
            jnp.bfloat16
        )
        for j in range(blocks)
    ]

    def keep(owner, at, value):
        slot = slot_of(owner, ids[1], len(plan))
        top, bottom = value[: LANES // CORES], value[LANES // CORES :]
        lanes = slice(at * LANES, (at + 1) * LANES)
        own_ref[slot, :, lanes] = jnp.where(first, top, bottom)
        mate_ref[slot, :, lanes] = jnp.where(first, bottom, top)

    spared = 0
    for tap in range(9):
        out = slice(tap * LANES, (tap + 1) * LANES)
        total = dot_nn(g_refs[0][out, :], deeps[0])
        for j in range(1, blocks):
            total = total + dot_nn(g_refs[j][out, :], deeps[j])
        if begun is not None:
            total = total + sum_ref[out, begun : begun + total.shape[1]]
        if not done:
            total_ref[out, :] = total
            continue
        for p, unit in enumerate(summed):
            value = total[:, p * LANES : (p + 1) * LANES]
            if (tap, unit) in places:
                keep(*places[tap, unit], value)
            else:
                extra_out[spared] = value
                spared += 1
    for ref, pairs in zip(extra_refs, late):
        for i, pair in enumerate(pairs):
            keep(*places[pair], ref[i])


def sum_kernel(plan, width, replicas, ids, *refs):
    *in_refs, out_ref = refs
    span = out_ref.shape[-1]
    for index, owners in enumerate(plan):
        parts = in_refs[index * replicas : (index + 1) * replicas]
        for i in range(len(owners[0])):
            lanes = slice(i * LANES, (i + 1) * LANES)
            value = parts[0][:, lanes]
            for ref in parts[1:]:
                value = value + ref[:, lanes]
            place = jnp.int32(0)
            for q, pairs in enumerate(owners):
                tap, unit = pairs[i]
                place = jnp.where(ids[1] == q, tap * width + unit * LANES - q * span, place)
            out_ref[0, :, pl.ds(pl.multiple_of(place, LANES), LANES)] = value


def on_device(images, filters, out_grad):
    count, rows, cols, chans = images.shape
    owned, kdim = filters.shape[1:]
    width = kdim // 9
    shards, replicas = lax.axis_size("shard"), lax.axis_size("replica")
    parts = shards // CORES
    ups, downs = parts // 2, (parts - 1) // 2
    span = kdim // replicas
    shape = (count, rows, cols)
    real = count * rows * LINE
    packed = -(-count * rows * cols // 8) * 8
    deep = 3 * (real // LANES * LANES) + -(-3 * (real % LANES) // LANES) * LANES
    chunks = chunk_units(width)
    plan = exchange_plan(width, replicas)
    f32 = functools.partial(jax.ShapeDtypeStruct, dtype=jnp.float32)
    bf16 = functools.partial(jax.ShapeDtypeStruct, dtype=jnp.bfloat16)

    ring = list(range(0, parts, 2)) + list(range(1, parts, 2))[::-1]
    table = [
        [s % CORES] + [ring[(ring.index(s // CORES) + d) % parts] for d in range(parts)]
        for s in range(shards)
    ]
    mine = lax.dynamic_index_in_dim(
        jnp.array(table, jnp.int32), lax.axis_index("shard"), 0, keepdims=False
    )
    rep = lax.axis_index("replica").astype(jnp.int32)
    ids = jnp.concatenate([mine[:1], rep[None], mine[1:]])

    def onward(value, d):
        return lax.ppermute(
            value,
            "shard",
            [(s, CORES * table[s][1 + d % parts] + s % CORES) for s in range(shards)],
        )

    def across(value):
        return lax.ppermute(value, "shard", [(s, s ^ 1) for s in range(shards)])

    order = []

    def ordered(kernel, name, out_shape, operands, **keywords):
        first = after(ids, *order[-1:])
        made = call(kernel, name, out_shape, [first, *operands], **keywords)
        order.append(made[0])
        return made

    mate_filters = across(filters)
    size0 = len(chunks[0])
    up, down, *rest, own_grad = ordered(
        functools.partial(pack_kernel, chunks, parts),
        "pack",
        [f32((size0 + n, packed, LANES)) for n in (ups, downs)]
        + [f32((len(c), packed, LANES)) for c in chunks[1:]]
        + [f32((1, packed, LANES))],
        [images, out_grad],
    )

    far = parts - ups
    near = [d for d in range(1, parts) if d != far]
    weights = ordered(
        functools.partial(filter_kernel, chunks),
        "prepare_filters",
        [bf16((9 * LANES, 3 * len(c) * LANES)) for c in chunks],
        [filters, mate_filters],
    )
    pad = [pltpu.VMEM((2 * LINE + count * (rows + 2) * LINE, LANES), jnp.float32)]

    def prepare_grad(blocks):
        return ordered(
            functools.partial(grad_kernel, shape),
            "prepare_grad",
            [bf16((9 * LANES, deep))] * len(blocks),
            blocks,
            scratch=pad,
        )

    def multiply(blocks, grads, summed, begun=None, at=None, late=(), extras=(), done=None, convolve=True):
        units = [chunks[i] for i in (range(len(chunks)) if convolve else summed)]
        lanes = [u for i in summed for u in chunks[i]]
        size = sum(len(c) for c in units) * LANES
        out_shape = [f32((packed, LANES))] * len(blocks) if convolve else []
        if done is None:
            out_shape.append(f32((9 * LANES, len(lanes) * LANES)))
        else:
            out_shape += [f32((replicas, owned, len(plan[done][0]) * LANES))] * 2
            if late and not convolve:
                out_shape.append(f32((len(late), LANES, LANES)))
        operands = [piece for block in blocks for piece in block] + list(grads)
        operands += weights if convolve else []
        operands += [begun] if begun is not None else []
        scratch = [pltpu.VMEM((len(blocks) * real, size), jnp.float32)]
        if convolve:
            scratch.append(pltpu.VMEM((len(blocks) * real, 9 * LANES), jnp.float32))
        made = ordered(
            functools.partial(
                multiply_kernel,
                shape,
                units,
                lanes,
                [] if done is None else plan[done],
                late,
                len(blocks),
                at,
                done is not None,
                convolve,
            ),
            "multiply",
            out_shape,
            operands + list(extras),
            scratch=scratch,
        )
        outputs = len(blocks) if convolve else 0
        return made[:outputs], made[outputs:]

    everything = list(range(len(chunks)))
    grads = [None] * parts
    (grads[0],) = prepare_grad([own_grad])
    (own_conv,), (total,) = multiply([[up, *rest]], grads[:1], everything)

    sent_up, sent_down = [up, *rest], [down, *rest]
    gathered = [None] * parts
    for step in range(1, ups + 1):
        if step <= downs:
            sent_down = [onward(value, -1) for value in sent_down]
            gathered[step] = sent_down
            sent_down = [sent_down[0][:-1], *sent_down[1:]]
        if step < ups:
            sent_up = [onward(value, 1) for value in sent_up]
            gathered[parts - step] = sent_up
            if step + 1 == ups:
                sent_up[0] = after(sent_up[0], total, *sent_up[1:], *sent_down[1:])
            sent_up = [sent_up[0][:-1], *sent_up[1:]]
    near = [d for d in range(1, parts) if d != parts - ups]
    far = parts - ups
    gathered[far] = [onward(sent_up[0], 1)]
    returned = [own_conv] + [None] * (parts - 1)
    if near:
        for d, grad in zip(near, prepare_grad([gathered[d][0] for d in near])):
            grads[d] = grad
        outputs, (total,) = multiply(
            [gathered[d] for d in near], [grads[d] for d in near], everything, total, 0
        )
        for d, value in zip(near, outputs):
            returned[d] = onward(value, d)
        sent_up = sent_up[:1] + [after(value, total) for value in sent_up[1:]]
    gathered[far] += [onward(value, 1) for value in sent_up[1:]]

    (grads[far],) = prepare_grad([gathered[far][0]])
    extras, late, sums = [], [], []
    for index, chunk in enumerate(chunks):
        final = index + 1 == len(chunks)
        carried = {pair for pairs in plan[index] for pair in pairs}
        spare = [(t, u) for t in range(9) for u in chunk if (t, u) not in carried]
        outputs, (own, mate, *spared) = multiply(
            [gathered[far] if final else [gathered[far][index]]],
            [grads[far]],
            [index],
            total,
            chunk[0] * LANES,
            late if final else spare,
            extras if final else (),
            index,
            final,
        )
        if final:
            returned[far] = onward(outputs[0], far)
        extras += spared
        if spare:
            late.append(spare)
        both = own + across(mate)
        sums.append(both[0])
        for step in range(1, replicas):
            sums.append(
                lax.ppermute(
                    both[step],
                    "replica",
                    [(r, partner(r, step, replicas)) for r in range(replicas)],
                )
            )

    (conv_out,) = ordered(
        functools.partial(join_kernel, parts),
        "join_output",
        [f32(images.shape)],
        returned,
    )
    (filter_grad,) = ordered(
        functools.partial(sum_kernel, plan, width, replicas),
        "sum_replicas",
        [f32((1, owned, span))],
        sums,
    )
    return conv_out, filter_grad


def solution(mesh):
    return jax.shard_map(
        on_device,
        mesh=mesh,
        in_specs=(
            P(("replica", "shard"), None, None, None),
            P(None, "shard", None),
            P(("replica", "shard"), None, None, None),
        ),
        out_specs=(P(("replica", "shard"), None, None, None), P(None, "shard", "replica")),
        check_vma=False,
    )
```

profile of v0, /device:TPU:0, one launch (start us, length us, event | category | flops | bytes accessed | tf_op | source)
XLA Modules:
  0.0 65.7 jit_solution(8270877752203781176)
XLA Ops:
  1.1 0.7 %constant_dynamic-slice_fusion = s32[1,5]{1,0:T(1,128)S(1)} fusion(s32[8,5]{1,0:T(8,128)} %constant.16.clone, s32[]{:T(128)S(6)} %select_n.4), kind=kLoop, calls=%fused_computation.10 | loop fusion | bytes 44 | tf_op jit(solution)/shard_map/jit(dynamic_index_in_dim)/dynamic_slice | solution.py:359
  2.0 1.0 %copy-done.1 = f32[3,7,7,512]{3,2,1,0:T(8,128)S(1)} copy-done((f32[3,7,7,512]{3,2,1,0:T(8,128)S(1)}, f32[3,7,7,512]{3,2,1,0:T(8,128)}, u32[]{:S(2)}) %copy-start.1) | copy-done | bytes 301080
  3.0 1.0 %copy-done.2 = f32[3,7,7,512]{3,2,1,0:T(8,128)S(1)} copy-done((f32[3,7,7,512]{3,2,1,0:T(8,128)S(1)}, f32[3,7,7,512]{3,2,1,0:T(8,128)}, u32[]{:S(2)}) %copy-start.2) | copy-done | bytes 301080
  4.0 0.6 pack.1
  4.6 3.7 %collective-permute-start.2 = (f32[4,152,128]{2,1,0:T(8,128)S(1)}, f32[4,152,128]{2,1,0:T(8,128)S(1)}, u32[]{:S(2)}, u32[]{:S(2)}) collective-permute-start(f32[4,152,128]{2,1,0:T(8,128)S(1)} %get-tuple-element.33.refs_0_), channel_id=1, source_target_pairs={{0,4},{1,5},{2,0},{3,1},{4,6},{5,7},{6,2},{7,3},{8,12},{9,13},{10,... | collective-permute-start | bytes 933896 | tf_op jit(solution)/shard_map/ppermute | solution.py:366
  8.3 1.6 %collective-permute-start.3 = (f32[2,152,128]{2,1,0:T(8,128)S(1)}, f32[2,152,128]{2,1,0:T(8,128)S(1)}, u32[]{:S(2)}, u32[]{:S(2)}) collective-permute-start(f32[2,152,128]{2,1,0:T(8,128)S(1)} %get-tuple-element.39.refs_1_), channel_id=1, source_target_pairs={{0,4},{1,5},{2,0},{3,1},{4,6},{5,7},{6,2},{7,3},{8,12},{9,13},{10,... | collective-permute-start | bytes 466952 | tf_op jit(solution)/shard_map/ppermute | solution.py:366
  10.3 1.3 %copy-done = f32[1,64,4608]{2,1,0:T(8,128)S(1)} copy-done((f32[1,64,4608]{2,1,0:T(8,128)S(1)}, f32[1,64,4608]{2,1,0:T(8,128)}, u32[]{:S(2)}) %copy-start) | copy-done | bytes 1179672
  11.6 1.0 %prepare_filters.1 = (bf16[1152,768]{1,0:T(8,128)(2,1)S(1)}, bf16[1152,768]{1,0:T(8,128)(2,1)S(1)}) custom-call(s32[6]{0:T(128)S(1)} %pad_add_fusion.ids, f32[1,64,4608]{2,1,0:T(8,128)S(1)} %copy-done, f32[1,64,4608]{2,1,0:T(8,128)S(1)} %collective-permute-done.mate_ref), custom_call_target="tpu_custom_call" | custom-call | tf_op jit(solution)/shard_map/prepare_filters/pallas_call | solution.py:19
  12.6 0.9 %prepare_grad.3.refs_2_ = bf16[1152,512]{1,0:T(8,128)(2,1)S(1)} custom-call(s32[6]{0:T(128)S(1)} %pad_add_fusion.ids, f32[1,152,128]{2,1,0:T(8,128)S(1)} %get-tuple-element.37.refs_0_), custom_call_target="tpu_custom_call" | custom-call | tf_op jit(solution)/shard_map/prepare_grad/pallas_call | solution.py:19
  13.5 2.5 %multiply.4 = (f32[152,128]{1,0:T(8,128)S(1)}, f32[1152,512]{1,0:T(8,128)S(1)}) custom-call(s32[6]{0:T(128)S(1)} %pad_add_fusion.ids, f32[4,152,128]{2,1,0:T(8,128)S(1)} %get-tuple-element.33.refs_0_, f32[2,152,128]{2,1,0:T(8,128)S(1)} %get-tuple-element.39.refs_1_, bf16[1152,512]{1,0:T(8,128)(2,1)S(1)} %prepare_grad.3.refs_2_, ...), custom_call_target="tpu_custom_call" | custom-call | tf_op jit(solution)/shard_map/multiply/pallas_call | solution.py:19
  16.0 3.4 %collective-permute-done.3.refs_3_ = f32[2,152,128]{2,1,0:T(8,128)S(1)} collective-permute-done((f32[2,152,128]{2,1,0:T(8,128)S(1)}, f32[2,152,128]{2,1,0:T(8,128)S(1)}, u32[]{:S(2)}, u32[]{:S(2)}) %collective-permute-start.3) | collective-permute-done | bytes 155680 | tf_op jit(solution)/shard_map/ppermute | solution.py:366
  19.3 4.8 %collective-permute-done.4.refs_1_ = f32[2,152,128]{2,1,0:T(8,128)S(1)} collective-permute-done((f32[2,152,128]{2,1,0:T(8,128)S(1)}, f32[2,152,128]{2,1,0:T(8,128)S(1)}, u32[]{:S(2)}, u32[]{:S(2)}) %collective-permute-start.4) | collective-permute-done | bytes 155680 | tf_op jit(solution)/shard_map/ppermute | solution.py:366
  24.2 1.0 %collective-permute-start.5 = (f32[3,152,128]{2,1,0:T(8,128)S(1)}, f32[3,152,128]{2,1,0:T(8,128)S(1)}, u32[]{:S(2)}, u32[]{:S(2)}) collective-permute-start(f32[3,152,128]{2,1,0:T(8,128)S(1)} %slice.43), channel_id=1, source_target_pairs={{0,4},{1,5},{2,0},{3,1},{4,6},{5,7},{6,2},{7,3},{8,12},{9,13},{10,... | collective-permute-start | bytes 700424 | tf_op jit(solution)/shard_map/ppermute | solution.py:366
  25.1 4.4 %collective-permute-done.1.refs_0_ = f32[3,152,128]{2,1,0:T(8,128)S(1)} collective-permute-done((f32[3,152,128]{2,1,0:T(8,128)S(1)}, f32[3,152,128]{2,1,0:T(8,128)S(1)}, u32[]{:S(2)}, u32[]{:S(2)}) %collective-permute-start.1) | collective-permute-done | bytes 233504 | tf_op jit(solution)/shard_map/ppermute | solution.py:366
  29.5 1.1 %prepare_grad.4 = (bf16[1152,512]{1,0:T(8,128)(2,1)S(1)}, bf16[1152,512]{1,0:T(8,128)(2,1)S(1)}) custom-call(s32[6]{0:T(128)S(1)} %pad_add_fusion.ids, f32[3,152,128]{2,1,0:T(8,128)S(1)} %collective-permute-done.1.refs_0_, f32[4,152,128]{2,1,0:T(8,128)S(1)} %collective-permute-done.2.refs_1_.refs_2_), custom_call_target="tpu_custom_call" | custom-call | tf_op jit(solution)/shard_map/prepare_grad/pallas_call | solution.py:19
  30.6 3.4 %multiply.5 = (f32[152,128]{1,0:T(8,128)S(1)}, f32[152,128]{1,0:T(8,128)S(1)}, f32[1152,512]{1,0:T(8,128)S(1)}) custom-call(s32[6]{0:T(128)S(1)} %pad_add_fusion.ids, f32[3,152,128]{2,1,0:T(8,128)S(1)} %collective-permute-done.1.refs_0_, f32[2,152,128]{2,1,0:T(8,128)S(1)} %collective-permute-done.4.refs_1_, ...), custom_call_target="tpu_custom_call" | custom-call | tf_op jit(solution)/shard_map/multiply/pallas_call | solution.py:19
  34.0 0.6 collective-permute-start.6
  34.6 0.9 %prepare_grad.5.refs_1_.refs_2_ = bf16[1152,512]{1,0:T(8,128)(2,1)S(1)} custom-call(s32[6]{0:T(128)S(1)} %pad_add_fusion.ids, f32[3,152,128]{2,1,0:T(8,128)S(1)} %collective-permute-done.5.refs_0_), custom_call_target="tpu_custom_call" | custom-call | tf_op jit(solution)/shard_map/prepare_grad/pallas_call | solution.py:19
  35.5 1.1 %multiply.6 = (f32[4,64,512]{2,1,0:T(8,128)S(1)}, f32[4,64,512]{2,1,0:T(8,128)S(1)}, f32[2,128,128]{2,1,0:T(8,128)S(1)}) custom-call(s32[6]{0:T(128)S(1)} %pad_add_fusion.ids, f32[3,152,128]{2,1,0:T(8,128)S(1)} %collective-permute-done.5.refs_0_, bf16[1152,512]{1,0:T(8,128)(2,1)S(1)} %prepare_grad.5.refs_1_.refs_2_, ...), custom_call_target="tpu_custom_call" | custom-call | tf_op jit(solution)/shard_map/multiply/pallas_call | solution.py:19
  36.7 3.2 %collective-permute-done.6.refs_1_ = f32[2,152,128]{2,1,0:T(8,128)S(1)} collective-permute-done((f32[2,152,128]{2,1,0:T(8,128)S(1)}, f32[2,152,128]{2,1,0:T(8,128)S(1)}, u32[]{:S(2)}, u32[]{:S(2)}) %collective-permute-start.6) | collective-permute-done | bytes 155680 | tf_op jit(solution)/shard_map/ppermute | solution.py:366
  39.9 2.2 %multiply.7 = (f32[152,128]{1,0:T(8,128)S(1)}, f32[4,64,640]{2,1,0:T(8,128)S(1)}, f32[4,64,640]{2,1,0:T(8,128)S(1)}) custom-call(s32[6]{0:T(128)S(1)} %pad_add_fusion.ids, f32[3,152,128]{2,1,0:T(8,128)S(1)} %collective-permute-done.5.refs_0_, f32[2,152,128]{2,1,0:T(8,128)S(1)} %collective-permute-done.6.refs_1_, ...), custom_call_target="tpu_custom_call" | custom-call | tf_op jit(solution)/shard_map/multiply/pallas_call | solution.py:19
  42.2 1.2 %collective-permute-start.7 = (f32[152,128]{1,0:T(8,128)S(1)}, f32[152,128]{1,0:T(8,128)S(1)}, u32[]{:S(2)}, u32[]{:S(2)}) collective-permute-start(f32[152,128]{1,0:T(8,128)S(1)} %get-tuple-element.49), channel_id=1, source_target_pairs={{0,4},{1,5},{2,0},{3,1},{4,6},{5,7},{6,2},{7,3},{8,12},{9,13},{10,... | collective-permute-start | bytes 233480 | tf_op jit(solution)/shard_map/ppermute | solution.py:366
  43.4 0.8 %collective-permute-start.9 = (f32[152,128]{1,0:T(8,128)S(1)}, f32[152,128]{1,0:T(8,128)S(1)}, u32[]{:S(2)}, u32[]{:S(2)}) collective-permute-start(f32[152,128]{1,0:T(8,128)S(1)} %get-tuple-element.59), channel_id=1, source_target_pairs={{0,2},{1,3},{2,6},{3,7},{4,0},{5,1},{6,4},{7,5},{8,10},{9,11},{10,... | collective-permute-start | bytes 233480 | tf_op jit(solution)/shard_map/ppermute | solution.py:366
  44.3 2.5 %collective-permute-start.8 = (f32[152,128]{1,0:T(8,128)S(1)}, f32[152,128]{1,0:T(8,128)S(1)}, u32[]{:S(2)}, u32[]{:S(2)}) collective-permute-start(f32[152,128]{1,0:T(8,128)S(1)} %get-tuple-element.57), channel_id=1, source_target_pairs={{0,6},{1,7},{2,4},{3,5},{4,2},{5,3},{6,0},{7,1},{8,14},{9,15},{10,... | collective-permute-start | bytes 233480 | tf_op jit(solution)/shard_map/ppermute | solution.py:366
  46.9 1.5 %collective-permute-start.11 = (f32[64,512]{1,0:T(8,128)S(1)}, f32[64,512]{1,0:T(8,128)S(1)}, u32[]{:S(2)}, u32[]{:S(2)}) collective-permute-start(f32[64,512]{1,0:T(8,128)S(1)} %get-tuple-element.70), channel_id=1, source_target_pairs={{0,8},{8,0},{16,24},{24,16},{1,9},{9,1},{17,25},{25,17},{2,10},{10... | collective-permute-start | bytes 393224 | tf_op jit(solution)/shard_map/ppermute | solution.py:510
  48.6 0.7 %collective-permute-start.15 = (f32[64,640]{1,0:T(8,128)S(1)}, f32[64,640]{1,0:T(8,128)S(1)}, u32[]{:S(2)}, u32[]{:S(2)}) collective-permute-start(f32[64,640]{1,0:T(8,128)S(1)} %get-tuple-element.66), channel_id=1, source_target_pairs={{0,8},{8,0},{16,24},{24,16},{1,9},{9,1},{17,25},{25,17},{2,10},{10... | collective-permute-start | bytes 491528 | tf_op jit(solution)/shard_map/ppermute | solution.py:510
  49.3 1.5 %collective-permute-start.16 = (f32[64,640]{1,0:T(8,128)S(1)}, f32[64,640]{1,0:T(8,128)S(1)}, u32[]{:S(2)}, u32[]{:S(2)}) collective-permute-start(f32[64,640]{1,0:T(8,128)S(1)} %get-tuple-element.65), channel_id=1, source_target_pairs={{0,16},{8,24},{16,0},{24,8},{1,17},{9,25},{17,1},{25,9},{2,18},{10... | collective-permute-start | bytes 491528 | tf_op jit(solution)/shard_map/ppermute | solution.py:510
  50.8 2.4 %collective-permute-start.17 = (f32[64,640]{1,0:T(8,128)S(1)}, f32[64,640]{1,0:T(8,128)S(1)}, u32[]{:S(2)}, u32[]{:S(2)}) collective-permute-start(f32[64,640]{1,0:T(8,128)S(1)} %get-tuple-element.64), channel_id=1, source_target_pairs={{0,24},{8,16},{16,8},{24,0},{1,25},{9,17},{17,9},{25,1},{2,26},{10... | collective-permute-start | bytes 491528 | tf_op jit(solution)/shard_map/ppermute | solution.py:510
  53.8 2.1 %collective-permute-start.13 = (f32[64,512]{1,0:T(8,128)S(1)}, f32[64,512]{1,0:T(8,128)S(1)}, u32[]{:S(2)}, u32[]{:S(2)}) collective-permute-start(f32[64,512]{1,0:T(8,128)S(1)} %get-tuple-element.68), channel_id=1, source_target_pairs={{0,24},{8,16},{16,8},{24,0},{1,25},{9,17},{17,9},{25,1},{2,26},{10... | collective-permute-start | bytes 393224 | tf_op jit(solution)/shard_map/ppermute | solution.py:510
  55.8 1.3 %join_output.1 = f32[3,7,7,512]{3,2,1,0:T(8,128)} custom-call(s32[6]{0:T(128)S(1)} %pad_add_fusion.ids, f32[152,128]{1,0:T(8,128)S(1)} %get-tuple-element.41.refs_0_, f32[152,128]{1,0:T(8,128)S(1)} %collective-permute-done.7.refs_1_, f32[152,128]{1,0:T(8,128)S(1)} %collective-permute-done.8.refs_2_, f32[152,128]{1,0:T(8,128)S(1)} %collective-permute-done.9.refs_3_), custom_call_target="tpu_custom_call" | custom-call | tf_op jit(solution)/shard_map/join_output/pallas_call | solution.py:19
  57.1 7.2 %collective-permute-done.12.refs_2_ = f32[64,512]{1,0:T(8,128)S(1)} collective-permute-done((f32[64,512]{1,0:T(8,128)S(1)}, f32[64,512]{1,0:T(8,128)S(1)}, u32[]{:S(2)}, u32[]{:S(2)}) %collective-permute-start.12) | collective-permute-done | bytes 131104 | tf_op jit(solution)/shard_map/ppermute | solution.py:510
  64.4 1.3 %sum_replicas.1 = f32[1,64,1152]{2,1,0:T(8,128)} custom-call(s32[6]{0:T(128)S(1)} %pad_add_fusion.ids, f32[64,512]{1,0:T(8,128)S(1)} %get-tuple-element.71.refs_0_, f32[64,512]{1,0:T(8,128)S(1)} %collective-permute-done.11.refs_1_, f32[64,512]{1,0:T(8,128)S(1)} %collective-permute-done.12.refs_2_, f32[64,512]{1,0:T(8,128)S(1)} %collective-permute-done.13.refs_3_, ...), custom_call_target="tpu_custom_call" | custom-call | tf_op jit(solution)/shard_map/sum_replicas/pallas_call | solution.py:19
  (29 shorter events, 2.3 us)
Async XLA Ops:
  0.6 9.7 %collective-permute-start = (f32[1,64,4608]{2,1,0:T(8,128)}, f32[1,64,4608]{2,1,0:T(8,128)S(1)}, u32[]{:S(2)}, u32[]{:S(2)}) collective-permute-start(f32[1,64,4608]{2,1,0:T(8,128)} %own_ref.1), channel_id=1, source_target_pairs={{0,1},{1,0},{2,3},{3,2},{4,5},{5,4},{6,7},{7,6},{8,9},{9,8},{10,11... | collective-permute-start | bytes 3538952 | tf_op jit(solution)/shard_map/ppermute | solution.py:373
  2.0 1.0 %copy-start.1 = (f32[3,7,7,512]{3,2,1,0:T(8,128)S(1)}, f32[3,7,7,512]{3,2,1,0:T(8,128)}, u32[]{:S(2)}) copy-start(f32[3,7,7,512]{3,2,1,0:T(8,128)} %image_ref.1) | copy-start | bytes 903172
  3.0 1.0 %copy-start.2 = (f32[3,7,7,512]{3,2,1,0:T(8,128)S(1)}, f32[3,7,7,512]{3,2,1,0:T(8,128)}, u32[]{:S(2)}) copy-start(f32[3,7,7,512]{3,2,1,0:T(8,128)} %grad_ref.1) | copy-start | bytes 903172
  4.6 19.5 %collective-permute-start.2 = (f32[4,152,128]{2,1,0:T(8,128)S(1)}, f32[4,152,128]{2,1,0:T(8,128)S(1)}, u32[]{:S(2)}, u32[]{:S(2)}) collective-permute-start(f32[4,152,128]{2,1,0:T(8,128)S(1)} %get-tuple-element.33.refs_0_), channel_id=1, source_target_pairs={{0,4},{1,5},{2,0},{3,1},{4,6},{5,7},{6,2},{7,3},{8,12},{9,13},{10,... | collective-permute-start | bytes 933896 | tf_op jit(solution)/shard_map/ppermute | solution.py:366
  8.3 11.1 %collective-permute-start.3 = (f32[2,152,128]{2,1,0:T(8,128)S(1)}, f32[2,152,128]{2,1,0:T(8,128)S(1)}, u32[]{:S(2)}, u32[]{:S(2)}) collective-permute-start(f32[2,152,128]{2,1,0:T(8,128)S(1)} %get-tuple-element.39.refs_1_), channel_id=1, source_target_pairs={{0,4},{1,5},{2,0},{3,1},{4,6},{5,7},{6,2},{7,3},{8,12},{9,13},{10,... | collective-permute-start | bytes 466952 | tf_op jit(solution)/shard_map/ppermute | solution.py:366
  9.9 14.3 %collective-permute-start.4 = (f32[2,152,128]{2,1,0:T(8,128)S(1)}, f32[2,152,128]{2,1,0:T(8,128)S(1)}, u32[]{:S(2)}, u32[]{:S(2)}) collective-permute-start(f32[2,152,128]{2,1,0:T(8,128)S(1)} %get-tuple-element.39.refs_1_), channel_id=1, source_target_pairs={{0,2},{1,3},{2,6},{3,7},{4,0},{5,1},{6,4},{7,5},{8,10},{9,11},{10,... | collective-permute-start | bytes 466952 | tf_op jit(solution)/shard_map/ppermute | solution.py:366
  10.3 19.2 %collective-permute-start.1 = (f32[3,152,128]{2,1,0:T(8,128)S(1)}, f32[3,152,128]{2,1,0:T(8,128)S(1)}, u32[]{:S(2)}, u32[]{:S(2)}) collective-permute-start(f32[3,152,128]{2,1,0:T(8,128)S(1)} %get-tuple-element.43), channel_id=1, source_target_pairs={{0,2},{1,3},{2,6},{3,7},{4,0},{5,1},{6,4},{7,5},{8,10},{9,11},{10,... | collective-permute-start | bytes 700424 | tf_op jit(solution)/shard_map/ppermute | solution.py:366
  10.3 1.3 %copy-start = (f32[1,64,4608]{2,1,0:T(8,128)S(1)}, f32[1,64,4608]{2,1,0:T(8,128)}, u32[]{:S(2)}) copy-start(f32[1,64,4608]{2,1,0:T(8,128)} %own_ref.1) | copy-start | bytes 3538948
  24.2 10.5 %collective-permute-start.5 = (f32[3,152,128]{2,1,0:T(8,128)S(1)}, f32[3,152,128]{2,1,0:T(8,128)S(1)}, u32[]{:S(2)}, u32[]{:S(2)}) collective-permute-start(f32[3,152,128]{2,1,0:T(8,128)S(1)} %slice.43), channel_id=1, source_target_pairs={{0,4},{1,5},{2,0},{3,1},{4,6},{5,7},{6,2},{7,3},{8,12},{9,13},{10,... | collective-permute-start | bytes 700424 | tf_op jit(solution)/shard_map/ppermute | solution.py:366
  34.0 5.9 %collective-permute-start.6 = (f32[2,152,128]{2,1,0:T(8,128)S(1)}, f32[2,152,128]{2,1,0:T(8,128)S(1)}, u32[]{:S(2)}, u32[]{:S(2)}) collective-permute-start(f32[2,152,128]{2,1,0:T(8,128)S(1)} %collective-permute-done.3.refs_3_), channel_id=1, source_target_pairs={{0,4},{1,5},{2,0},{3,1},{4,6},{5,7},{6,2},{7,3},{8,12},{9,13},{10,... | collective-permute-start | bytes 466952 | tf_op jit(solution)/shard_map/ppermute | solution.py:366
  36.6 10.2 %collective-permute-start.10 = (f32[4,64,512]{2,1,0:T(8,128)S(1)}, f32[4,64,512]{2,1,0:T(8,128)S(1)}, u32[]{:S(2)}, u32[]{:S(2)}) collective-permute-start(f32[4,64,512]{2,1,0:T(8,128)S(1)} %get-tuple-element.61), channel_id=1, source_target_pairs={{0,1},{1,0},{2,3},{3,2},{4,5},{5,4},{6,7},{7,6},{8,9},{9,8},{10,11... | collective-permute-start | bytes 1572872 | tf_op jit(solution)/shard_map/ppermute | solution.py:373
  42.1 6.3 %collective-permute-start.14 = (f32[4,64,640]{2,1,0:T(8,128)S(1)}, f32[4,64,640]{2,1,0:T(8,128)S(1)}, u32[]{:S(2)}, u32[]{:S(2)}) collective-permute-start(f32[4,64,640]{2,1,0:T(8,128)S(1)} %get-tuple-element.63), channel_id=1, source_target_pairs={{0,1},{1,0},{2,3},{3,2},{4,5},{5,4},{6,7},{7,6},{8,9},{9,8},{10,11... | collective-permute-start | bytes 1966088 | tf_op jit(solution)/shard_map/ppermute | solution.py:373
  42.2 7.0 %collective-permute-start.7 = (f32[152,128]{1,0:T(8,128)S(1)}, f32[152,128]{1,0:T(8,128)S(1)}, u32[]{:S(2)}, u32[]{:S(2)}) collective-permute-start(f32[152,128]{1,0:T(8,128)S(1)} %get-tuple-element.49), channel_id=1, source_target_pairs={{0,4},{1,5},{2,0},{3,1},{4,6},{5,7},{6,2},{7,3},{8,12},{9,13},{10,... | collective-permute-start | bytes 233480 | tf_op jit(solution)/shard_map/ppermute | solution.py:366
  43.4 7.4 %collective-permute-start.9 = (f32[152,128]{1,0:T(8,128)S(1)}, f32[152,128]{1,0:T(8,128)S(1)}, u32[]{:S(2)}, u32[]{:S(2)}) collective-permute-start(f32[152,128]{1,0:T(8,128)S(1)} %get-tuple-element.59), channel_id=1, source_target_pairs={{0,2},{1,3},{2,6},{3,7},{4,0},{5,1},{6,4},{7,5},{8,10},{9,11},{10,... | collective-permute-start | bytes 233480 | tf_op jit(solution)/shard_map/ppermute | solution.py:366
  44.3 9.0 %collective-permute-start.8 = (f32[152,128]{1,0:T(8,128)S(1)}, f32[152,128]{1,0:T(8,128)S(1)}, u32[]{:S(2)}, u32[]{:S(2)}) collective-permute-start(f32[152,128]{1,0:T(8,128)S(1)} %get-tuple-element.57), channel_id=1, source_target_pairs={{0,6},{1,7},{2,4},{3,5},{4,2},{5,3},{6,0},{7,1},{8,14},{9,15},{10,... | collective-permute-start | bytes 233480 | tf_op jit(solution)/shard_map/ppermute | solution.py:366
  46.9 6.8 %collective-permute-start.11 = (f32[64,512]{1,0:T(8,128)S(1)}, f32[64,512]{1,0:T(8,128)S(1)}, u32[]{:S(2)}, u32[]{:S(2)}) collective-permute-start(f32[64,512]{1,0:T(8,128)S(1)} %get-tuple-element.70), channel_id=1, source_target_pairs={{0,8},{8,0},{16,24},{24,16},{1,9},{9,1},{17,25},{25,17},{2,10},{10... | collective-permute-start | bytes 393224 | tf_op jit(solution)/shard_map/ppermute | solution.py:510
  48.6 15.8 %collective-permute-start.15 = (f32[64,640]{1,0:T(8,128)S(1)}, f32[64,640]{1,0:T(8,128)S(1)}, u32[]{:S(2)}, u32[]{:S(2)}) collective-permute-start(f32[64,640]{1,0:T(8,128)S(1)} %get-tuple-element.66), channel_id=1, source_target_pairs={{0,8},{8,0},{16,24},{24,16},{1,9},{9,1},{17,25},{25,17},{2,10},{10... | collective-permute-start | bytes 491528 | tf_op jit(solution)/shard_map/ppermute | solution.py:510
  49.3 15.1 %collective-permute-start.16 = (f32[64,640]{1,0:T(8,128)S(1)}, f32[64,640]{1,0:T(8,128)S(1)}, u32[]{:S(2)}, u32[]{:S(2)}) collective-permute-start(f32[64,640]{1,0:T(8,128)S(1)} %get-tuple-element.65), channel_id=1, source_target_pairs={{0,16},{8,24},{16,0},{24,8},{1,17},{9,25},{17,1},{25,9},{2,18},{10... | collective-permute-start | bytes 491528 | tf_op jit(solution)/shard_map/ppermute | solution.py:510
  50.8 13.5 %collective-permute-start.17 = (f32[64,640]{1,0:T(8,128)S(1)}, f32[64,640]{1,0:T(8,128)S(1)}, u32[]{:S(2)}, u32[]{:S(2)}) collective-permute-start(f32[64,640]{1,0:T(8,128)S(1)} %get-tuple-element.64), channel_id=1, source_target_pairs={{0,24},{8,16},{16,8},{24,0},{1,25},{9,17},{17,9},{25,1},{2,26},{10... | collective-permute-start | bytes 491528 | tf_op jit(solution)/shard_map/ppermute | solution.py:510
  53.2 11.1 %collective-permute-start.12 = (f32[64,512]{1,0:T(8,128)S(1)}, f32[64,512]{1,0:T(8,128)S(1)}, u32[]{:S(2)}, u32[]{:S(2)}) collective-permute-start(f32[64,512]{1,0:T(8,128)S(1)} %get-tuple-element.69), channel_id=1, source_target_pairs={{0,16},{8,24},{16,0},{24,8},{1,17},{9,25},{17,1},{25,9},{2,18},{10... | collective-permute-start | bytes 393224 | tf_op jit(solution)/shard_map/ppermute | solution.py:510
  53.8 10.6 %collective-permute-start.13 = (f32[64,512]{1,0:T(8,128)S(1)}, f32[64,512]{1,0:T(8,128)S(1)}, u32[]{:S(2)}, u32[]{:S(2)}) collective-permute-start(f32[64,512]{1,0:T(8,128)S(1)} %get-tuple-element.68), channel_id=1, source_target_pairs={{0,24},{8,16},{16,8},{24,0},{1,25},{9,17},{17,9},{25,1},{2,26},{10... | collective-permute-start | bytes 393224 | tf_op jit(solution)/shard_map/ppermute | solution.py:510
where the time goes:
time: 66 us; the launch traced here: 65.7 us
  waiting for transfers between devices  23.1 us (35%)
  starting transfers between devices  21.1 us (32%)
  Pallas kernels  16.3 us (25%)
  local copies, waits for them, and re-layouts  4.09 us (6%)
  between operations  0.76 us (1%)
    pallas_call x11, Pallas kernels, call(): pl.pallas_call(kernel, out_shape=out_shape, in_specs=[SMEM] + [VMEM] * (l...  16.3 us
    ppermute x9, waiting for transfers between devices, onward(): lax.ppermute(value, 'shard', [(s, CORES * table[s][1 + d % parts] + s % C...  15.9 us
    ppermute x9, starting transfers between devices, onward(): lax.ppermute(value, 'shard', [(s, CORES * table[s][1 + d % parts] + s % C...  11.9 us
    ppermute x6, starting transfers between devices, on_device(): lax.ppermute(both[step], 'replica', [(r, partner(r, step, replicas)) for...  8.58 us
    ppermute x6, waiting for transfers between devices, on_device(): lax.ppermute(both[step], 'replica', [(r, partner(r, step, replicas)) for...  7.25 us
    unnamed x6, local copies, waits for them, and re-layouts  3.23 us
  transfers between devices with their start and end apart: 18, of which 6 were waited for; matrix products, arithmetic and copies ran while one was open for 2% of the time, Pallas kernels for 23%

commit v1 on v0

v1 whole, which is shorter than its diff:
```python
import functools

import jax
import jax.numpy as jnp
from jax import lax
from jax.experimental import pallas as pl
from jax.experimental.pallas import tpu as pltpu
from jax.sharding import PartitionSpec as P

CORES = 2
LANES = 128
LINE = 8
CHUNK_SHARES = (2, 2)
VMEM = pl.BlockSpec(memory_space=pltpu.VMEM)


def call(kernel, name, out_shape, operands, scratch=(), mib=24):
    return pl.pallas_call(
        kernel,
        out_shape=out_shape,
        in_specs=[VMEM] * len(operands),
        out_specs=[VMEM] * len(out_shape),
        scratch_shapes=list(scratch),
        compiler_params=pltpu.CompilerParams(vmem_limit_bytes=mib * 1024 * 1024),
        cost_estimate=pl.CostEstimate(flops=0, bytes_accessed=0, transcendentals=0),
        name=name,
    )(*operands)


def ring_of(parts):
    return list(range(0, parts, 2)) + list(range(1, parts, 2))[::-1]


def chip_at(parts, d):
    chip = lax.axis_index("shard") // CORES
    at = jnp.where(chip % 2 == 0, chip // 2, parts - (chip + 1) // 2)
    at = (at + d) % parts
    return jnp.where(at < (parts + 1) // 2, 2 * at, 2 * (parts - at) - 1)


def first_core():
    return lax.axis_index("shard") % CORES == 0


def chunk_units(width):
    units = width // LANES
    share = units // sum(CHUNK_SHARES)
    bounds = [0]
    for part in CHUNK_SHARES:
        bounds.append(bounds[-1] + part * share)
    bounds[-1] = units
    return [list(range(a, b)) for a, b in zip(bounds, bounds[1:])]


def exchange_plan(width, replicas):
    units = width // LANES
    span = 9 * units // replicas
    chunks = chunk_units(width)
    late = [[] for _ in range(replicas)]
    plan = []
    for index, chunk in enumerate(chunks):
        mine = [
            [(t, u) for t in range(9) for u in chunk if (t * units + u) // span == q]
            for q in range(replicas)
        ]
        if index + 1 < len(chunks):
            base = min(len(m) for m in mine)
            for q in range(replicas):
                late[q] += mine[q][base:]
                mine[q] = mine[q][:base]
        else:
            mine = [m + extra for m, extra in zip(mine, late)]
        plan.append(mine)
    return plan


def partner(rep, step, count):
    return (rep + step) % count if count & (count - 1) else rep ^ step


def slot_of(owner, rep, count):
    if count & (count - 1):
        return lax.rem(owner - rep + count, count)
    return jnp.bitwise_xor(jnp.int32(owner), rep)


def after(value, *others):
    return lax.optimization_barrier((value, *others))[0]


def split(value):
    high = value.astype(jnp.bfloat16).astype(jnp.float32)
    return high, value - high


def deep_rows(first, second, third):
    rows, lanes = first.shape
    full = rows // LANES * LANES
    pieces = [p[:full] for p in (first, second, third)] if full else []
    rest = 3 * (rows - full)
    if rest:
        pieces += [p[full:] for p in (first, second, third)]
        gap = -rest % LANES
        if gap:
            pieces.append(jnp.zeros((gap, lanes), jnp.float32))
    return jnp.concatenate(pieces, axis=0)


def dot_nt(lhs, rhs):
    return lax.dot_general(
        lhs, rhs, (((1,), (1,)), ((), ())), preferred_element_type=jnp.float32
    )


def dot_nn(lhs, rhs):
    return lax.dot_general(
        lhs, rhs, (((1,), (0,)), ((), ())), preferred_element_type=jnp.float32
    )


def pack_kernel(parts, image_ref, grad_ref, *refs):
    up_ref, down_ref, *grad_refs = refs
    count, rows, cols, width = image_ref.shape
    dense = count * rows * cols
    units = width // LANES
    spare = up_ref.shape[1] - dense

    def pack(src, lanes, targets):
        for b in range(count):
            for h in range(rows):
                at = (b * rows + h) * cols
                value = src[b, h, :, lanes]
                for ref, p in targets:
                    ref[p, at : at + cols, :] = value
        if spare:
            for ref, p in targets:
                ref[p, dense:, :] = jnp.zeros((spare, LANES), jnp.float32)

    for unit in range(units):
        pack(image_ref, pl.ds(unit * LANES, LANES), [(up_ref, unit), (down_ref, unit)])
    middle = [d for d in range(parts) if d not in (1, parts - 1)]
    for d in range(parts):
        start = pl.multiple_of(chip_at(parts, d) * LANES, LANES)
        if d == 1:
            target = (up_ref, units)
        elif d == parts - 1:
            target = (down_ref, units)
        else:
            target = (grad_refs[middle.index(d)], 0)
        pack(grad_ref, pl.ds(start, LANES), [target])


def join_kernel(parts, *refs):
    out_ref = refs[-1]
    count, rows, cols, width = out_ref.shape
    for d in range(parts):
        start = chip_at(parts, (parts - d) % parts) * LANES
        lanes = pl.ds(pl.multiple_of(start, LANES), LANES)
        for b in range(count):
            for h in range(rows):
                at = (b * rows + h) * cols
                out_ref[b, h, :, lanes] = refs[d][at : at + cols, :]


def filter_kernel(own_ref, mate_ref, out_ref):
    owned, kdim = own_ref.shape[1:]
    width = kdim // 9
    first = first_core()
    for tap in range(9):
        rows = slice(tap * 2 * owned, (tap + 1) * 2 * owned)
        own = own_ref[0, :, tap * width : (tap + 1) * width]
        mate = mate_ref[0, :, tap * width : (tap + 1) * width]
        both = jnp.concatenate(
            [jnp.where(first, own, mate), jnp.where(first, mate, own)], axis=0
        )
        high, low = split(both)
        high = high.astype(jnp.bfloat16)
        out_ref[rows, :width] = high
        out_ref[rows, width : 2 * width] = high
        out_ref[rows, 2 * width :] = low.astype(jnp.bfloat16)


def grad_kernel(shape, *refs):
    count, rows, cols = shape
    *refs, pad_ref = refs
    in_refs, out_refs = refs[: len(refs) // 2], refs[len(refs) // 2 :]
    block = (rows + 2) * LINE
    pad_ref[...] = jnp.zeros_like(pad_ref)
    for in_ref, out_ref in zip(in_refs, out_refs):
        piece = in_ref.shape[0] - 1
        for b in range(count):
            for h in range(rows):
                at = LINE + b * block + (h + 1) * LINE
                dense = (b * rows + h) * cols
                pad_ref[at : at + cols, :] = in_ref[piece, dense : dense + cols, :]
        for tap in range(9):
            a, c = tap // 3, tap % 3
            pieces = []
            for b in range(count):
                start = LINE + b * block + (2 - a) * LINE - (c - 1)
                pieces.append(pad_ref[start : start + rows * LINE, :])
            high, low = split(jnp.concatenate(pieces, axis=0))
            deep = deep_rows(high, high, low)
            out_ref[tap * LANES : (tap + 1) * LANES, :] = jnp.transpose(deep).astype(
                jnp.bfloat16
            )


def tap_products(shape, blocks, high, low, w_ref, conv_refs, y_ref):
    count, height, cols = shape
    block = height * LINE
    real = count * block
    high, low = high.astype(jnp.bfloat16), low.astype(jnp.bfloat16)
    packed = jnp.concatenate([high, low, high], axis=1)
    for start in range(0, 9 * LANES, 2 * LANES):
        out = slice(start, min(start + 2 * LANES, 9 * LANES))
        y_ref[:, out] = dot_nt(packed, w_ref[out, :])
    gap = jnp.zeros((LINE, LANES), jnp.float32)
    for j, conv_ref in enumerate(conv_refs):
        for b in range(count):
            at = j * real + b * block
            sums = []
            for c in range(3):
                above, middle, below = (
                    y_ref[at : at + block, (3 * a + c) * LANES : (3 * a + c + 1) * LANES]
                    for a in range(3)
                )
                sums.append(
                    middle
                    + jnp.concatenate([gap, above[:-LINE]], axis=0)
                    + jnp.concatenate([below[LINE:], gap], axis=0)
                )
            result = (
                sums[1]
                + pltpu.roll(sums[0], 1, axis=0)
                + pltpu.roll(sums[2], block - 1, axis=0)
            )
            for h in range(height):
                dense = (b * height + h) * cols
                conv_ref[dense : dense + cols, :] = result[h * LINE : h * LINE + cols]
        spare = conv_ref.shape[0] - count * height * cols
        if spare:
            conv_ref[count * height * cols :, :] = jnp.zeros((spare, LANES), jnp.float32)


def multiply_kernel(shape, units, blocks, convolve, summed, begun, plan, late, last, *refs):
    refs = list(refs)

    def take(k):
        return [refs.pop(0) for _ in range(k)]

    x_refs = take(blocks)
    w_refs = take(1 if convolve else 0)
    g_refs = take(blocks if summed else 0)
    sum_refs = take(1 if begun is not None else 0)
    extra_refs = take(len(late) if last else 0)
    conv_refs = take(blocks if convolve else 0)
    if plan:
        own_ref, mate_ref = take(2)
        extra_out = take(1)[0] if late and not last else None
    elif summed:
        (total_ref,) = take(1)
    rows_ref, *y_refs = refs
    count, height, cols = shape
    real = count * height * LINE

    rows_ref[...] = jnp.zeros_like(rows_ref)
    for j, ref in enumerate(x_refs):
        for p, unit in enumerate(units):
            for line in range(count * height):
                at = j * real + line * LINE
                rows_ref[at : at + cols, p * LANES : (p + 1) * LANES] = ref[
                    unit, line * cols : (line + 1) * cols, :
                ]
    high, low = split(rows_ref[...])
    if convolve:
        tap_products(shape, blocks, high, low, *w_refs, conv_refs, *y_refs)
    if not summed:
        return

    first = first_core()
    rep = lax.axis_index("replica")
    places = {pair: (q, i) for q, pairs in enumerate(plan) for i, pair in enumerate(pairs)}
    deeps = [
        deep_rows(*(v[j * real : (j + 1) * real] for v in (high, low, high))).astype(jnp.bfloat16)
        for j in range(blocks)
    ]

    def keep(owner, at, value):
        slot = slot_of(owner, rep, len(plan))
        top, bottom = value[: LANES // CORES], value[LANES // CORES :]
        lanes = slice(at * LANES, (at + 1) * LANES)
        own_ref[slot, :, lanes] = jnp.where(first, top, bottom)
        mate_ref[slot, :, lanes] = jnp.where(first, bottom, top)

    spared = 0
    for tap in range(9):
        out = slice(tap * LANES, (tap + 1) * LANES)
        total = dot_nn(g_refs[0][out, :], deeps[0])
        for j in range(1, blocks):
            total = total + dot_nn(g_refs[j][out, :], deeps[j])
        for ref in sum_refs:
            total = total + ref[out, begun : begun + total.shape[1]]
        if not plan:
            total_ref[out, :] = total
            continue
        for p, unit in enumerate(units):
            value = total[:, p * LANES : (p + 1) * LANES]
            if (tap, unit) in places:
                keep(*places[tap, unit], value)
            else:
                extra_out[spared] = value
                spared += 1
    for ref, pairs in zip(extra_refs, late):
        for i, pair in enumerate(pairs):
            keep(*places[pair], ref[i])


def sum_kernel(plan, width, replicas, *refs):
    *in_refs, out_ref = refs
    span = out_ref.shape[-1]
    rep = lax.axis_index("replica")
    for index, owners in enumerate(plan):
        parts = in_refs[index * replicas : (index + 1) * replicas]
        for i in range(len(owners[0])):
            lanes = slice(i * LANES, (i + 1) * LANES)
            value = parts[0][:, lanes]
            for ref in parts[1:]:
                value = value + ref[:, lanes]
            place = jnp.int32(0)
            for q, pairs in enumerate(owners):
                tap, unit = pairs[i]
                place = jnp.where(rep == q, tap * width + unit * LANES - q * span, place)
            out_ref[0, :, pl.ds(pl.multiple_of(place, LANES), LANES)] = value


def on_device(images, filters, out_grad):
    count, rows, cols, chans = images.shape
    owned, kdim = filters.shape[1:]
    width = kdim // 9
    shards, replicas = lax.axis_size("shard"), lax.axis_size("replica")
    parts = shards // CORES
    ups, downs = parts // 2, (parts - 1) // 2
    span = kdim // replicas
    shape = (count, rows, cols)
    real = count * rows * LINE
    packed = -(-count * rows * cols // 8) * 8
    deep = 3 * (real // LANES * LANES) + -(-3 * (real % LANES) // LANES) * LANES
    units = list(range(width // LANES))
    chunks = chunk_units(width)
    plan = exchange_plan(width, replicas)
    f32 = functools.partial(jax.ShapeDtypeStruct, dtype=jnp.float32)
    bf16 = functools.partial(jax.ShapeDtypeStruct, dtype=jnp.bfloat16)
    ring = ring_of(parts)

    def onward(value, d):
        def target(s):
            return CORES * ring[(ring.index(s // CORES) + d) % parts] + s % CORES

        return lax.ppermute(value, "shard", [(s, target(s)) for s in range(shards)])

    def across(value):
        return lax.ppermute(value, "shard", [(s, s ^ 1) for s in range(shards)])

    def to_replica(value, step):
        pairs = [(r, partner(r, step, replicas)) for r in range(replicas)]
        return lax.ppermute(value, "replica", pairs)

    order = []

    def ordered(kernel, name, out_shape, operands, **keywords):
        operands = [after(operands[0], *order[-1:]), *operands[1:]]
        made = call(kernel, name, out_shape, operands, **keywords)
        order.append(made[0])
        return made

    def prepare_grad(blocks):
        return ordered(
            functools.partial(grad_kernel, shape),
            "prepare_grad",
            [bf16((9 * LANES, deep))] * len(blocks),
            blocks,
            scratch=[pltpu.VMEM((2 * LINE + count * (rows + 2) * LINE, LANES), jnp.float32)],
        )

    def multiply(blocks, grads=(), total=None, convolve=True, done=None, late=(), extras=()):
        taken = units if done is None else chunks[done]
        out_shape = [f32((packed, LANES))] * len(blocks) if convolve else []
        last = done is not None and done + 1 == len(chunks)
        if done is not None:
            out_shape += [f32((replicas, owned, len(plan[done][0]) * LANES))] * 2
            if late and not last:
                out_shape.append(f32((len(late), LANES, LANES)))
        elif grads:
            out_shape.append(f32((9 * LANES, width)))
        operands = list(blocks) + ([weights] if convolve else []) + list(grads)
        operands += ([total] if total is not None else []) + list(extras)
        scratch = [pltpu.VMEM((len(blocks) * real, len(taken) * LANES), jnp.float32)]
        if convolve:
            scratch.append(pltpu.VMEM((len(blocks) * real, 9 * LANES), jnp.float32))
        made = ordered(
            functools.partial(
                multiply_kernel,
                shape,
                taken,
                len(blocks),
                convolve,
                bool(grads),
                None if total is None else taken[0] * LANES,
                [] if done is None else plan[done],
                late,
                last,
            ),
            "multiply",
            out_shape,
            operands,
            scratch=scratch,
        )
        outputs = len(blocks) if convolve else 0
        return made[:outputs], made[outputs:]

    mate_filters = across(filters)
    middle = [d for d in range(parts) if d not in (1, parts - 1)]
    up, down, *split_grads = ordered(
        functools.partial(pack_kernel, parts),
        "pack",
        [f32((len(units) + 1, packed, LANES))] * 2 + [f32((1, packed, LANES))] * len(middle),
        [images, out_grad],
    )
    grad_blocks = [None] * parts
    grad_blocks[0] = split_grads[0]
    for d, value in zip(middle[1:], split_grads[1:]):
        grad_blocks[parts - d] = onward(value, d)
    (weights,) = ordered(
        filter_kernel,
        "prepare_filters",
        [bf16((9 * LANES, 3 * width))],
        [filters, mate_filters],
    )
    grads = [None] * parts
    for d, grad in zip(middle, prepare_grad([grad_blocks[d] for d in middle])):
        grads[d] = grad
    (own_conv,), (total,) = multiply([up], grads[:1])

    blocks = [up] + [None] * (parts - 1)
    for step in range(1, ups + 1):
        up = onward(up, 1)
        blocks[parts - step] = up
        if step <= downs:
            down = onward(down, -1)
            blocks[step] = down
        if step == 1:
            up = after(up, total)
        up, down = up[: len(units)], down[: len(units)]
    far = parts - ups
    near = [d for d in range(1, parts) if d != far]
    ends = [d for d in (1, parts - 1) if grads[d] is None]
    for d, grad in zip(ends, prepare_grad([blocks[d] for d in ends])):
        grads[d] = grad
    returned = [own_conv] + [None] * (parts - 1)
    outputs, (total,) = multiply([blocks[d] for d in near], [grads[d] for d in near], total)
    for d, value in zip(near, outputs):
        returned[d] = value

    extras, late, sums, previous = [], [], [], []
    for index, chunk in enumerate(chunks):
        last = index + 1 == len(chunks)
        carried = {pair for pairs in plan[index] for pair in pairs}
        spare = [(t, u) for t in range(9) for u in chunk if (t, u) not in carried]
        _, (own, mate, *spared) = multiply(
            [blocks[far]],
            [grads[far]],
            total,
            convolve=False,
            done=index,
            late=late if last else spare,
            extras=extras if last else (),
        )
        extras += spared
        if spare:
            late.append(spare)
        both = own + across(mate)
        sums.append(both[0])
        arrived = []
        for step in range(1, replicas):
            value = both[step]
            if previous:
                value = after(value, previous[step - 1])
            arrived.append(to_replica(value, step))
        sums += arrived
        if last:
            order.append(both)
            (returned[far],), _ = multiply([blocks[far]])
            settled = previous[-1:]
        previous = arrived
    for d in near + [far]:
        returned[d] = onward(after(returned[d], *settled), d)

    (conv_out,) = ordered(
        functools.partial(join_kernel, parts),
        "join_output",
        [f32(images.shape)],
        returned,
    )
    (filter_grad,) = ordered(
        functools.partial(sum_kernel, plan, width, replicas),
        "sum_replicas",
        [f32((1, owned, span))],
        sums,
    )
    return conv_out, filter_grad


def solution(mesh):
    return jax.shard_map(
        on_device,
        mesh=mesh,
        in_specs=(
            P(("replica", "shard"), None, None, None),
            P(None, "shard", None),
            P(("replica", "shard"), None, None, None),
        ),
        out_specs=(P(("replica", "shard"), None, None, None), P(None, "shard", "replica")),
        check_vma=False,
    )
```

time: 66 us -> 68.2 us (1.033)
  waiting for transfers between devices: 23.1 us -> 32.4 us
  Pallas kernels: 16.3 us -> 10.5 us
  local copies, waits for them, and re-layouts: 4.09 us -> 3.33 us
    ppermute x15 -> x13, waiting for transfers between devices: 23.1 us -> 31.6 us  [the longest x7 28.4 us: onward(): return lax.ppermute(value, 'shard', [(s, target(s)) for s in range(shards)])]
    pallas_call x11, Pallas kernels: 16.3 us -> 10.5 us  [call(): pl.pallas_call(kernel, out_shape=out_shape, in_specs=[VMEM] * len(operand...]
    ppermute x15 -> x13, starting transfers between devices: 20.5 us -> 19.6 us  [the longest x7 11.3 us: onward(): return lax.ppermute(value, 'shard', [(s, target(s)) for s in range(shards)])]
    ppermute x3, waiting for transfers between devices: 0.01 us -> 0.81 us  [across(): return lax.ppermute(value, 'shard', [(s, s ^ 1) for s in range(shards)])]
    dynamic_slice x1 -> x0, local copies, waits for them, and re-layouts: 0.69 us -> none  [on_device(): lax.dynamic_index_in_dim(jnp.array(table, jnp.int32), lax.axis_index('sha...]
  transfers between devices with their start and end apart: 18 -> 16, of which waited for: 6 -> 6; matrix products, arithmetic and copies ran while one was open for 2% -> 0% of each run, Pallas kernels for 23% -> 14%
where the time goes in v1:
time: 68.2 us; the launch traced here: 67.9 us
  waiting for transfers between devices  32.4 us (48%)
  starting transfers between devices  20.8 us (30%)
  Pallas kernels  10.5 us (15%)
  local copies, waits for them, and re-layouts  3.33 us (5%)
  between operations  0.75 us (1%)
    ppermute x7, waiting for transfers between devices, onward(): return lax.ppermute(value, 'shard', [(s, target(s)) for s in range(shards)])  28.4 us
    ppermute x7, starting transfers between devices, onward(): return lax.ppermute(value, 'shard', [(s, target(s)) for s in range(shards)])  11.3 us
    pallas_call x11, Pallas kernels, call(): pl.pallas_call(kernel, out_shape=out_shape, in_specs=[VMEM] * len(operand...  10.5 us
    ppermute x6, starting transfers between devices, to_replica(): return lax.ppermute(value, 'replica', pairs)  8.38 us
    unnamed x6, local copies, waits for them, and re-layouts  3.23 us
    ppermute x6, waiting for transfers between devices, to_replica(): return lax.ppermute(value, 'replica', pairs)  3.12 us
  transfers between devices with their start and end apart: 16, of which 6 were waited for; matrix products, arithmetic and copies ran while one was open for 0% of the time, Pallas kernels for 14%

profile of v1, /device:TPU:0, one launch (start us, length us, event | category | flops | bytes accessed | tf_op | source)
XLA Modules:
  0.0 67.9 jit_solution(2692949443449596686)
XLA Ops:
  0.6 0.5 collective-permute-start
  1.1 1.0 %copy-done.1 = f32[3,7,7,512]{3,2,1,0:T(8,128)S(1)} copy-done((f32[3,7,7,512]{3,2,1,0:T(8,128)S(1)}, f32[3,7,7,512]{3,2,1,0:T(8,128)}, u32[]{:S(2)}) %copy-start.1) | copy-done | bytes 301080
  2.1 1.0 %copy-done.2 = f32[3,7,7,512]{3,2,1,0:T(8,128)S(1)} copy-done((f32[3,7,7,512]{3,2,1,0:T(8,128)S(1)}, f32[3,7,7,512]{3,2,1,0:T(8,128)}, u32[]{:S(2)}) %copy-start.2) | copy-done | bytes 301080
  3.2 3.7 %collective-permute-start.2 = (f32[5,152,128]{2,1,0:T(8,128)S(1)}, f32[5,152,128]{2,1,0:T(8,128)S(1)}, u32[]{:S(2)}, u32[]{:S(2)}) collective-permute-start(f32[5,152,128]{2,1,0:T(8,128)S(1)} %get-tuple-element.43.refs_0_), channel_id=1, source_target_pairs={{0,4},{1,5},{2,0},{3,1},{4,6},{5,7},{6,2},{7,3},{8,12},{9,13},{10,... | collective-permute-start | bytes 1167368 | tf_op jit(solution)/shard_map/ppermute | solution.py:360
  6.9 1.3 %collective-permute-start.1 = (f32[1,152,128]{2,1,0:T(8,128)S(1)}, f32[1,152,128]{2,1,0:T(8,128)S(1)}, u32[]{:S(2)}, u32[]{:S(2)}) collective-permute-start(f32[1,152,128]{2,1,0:T(8,128)S(1)} %get-tuple-element.41), channel_id=1, source_target_pairs={{0,6},{1,7},{2,4},{3,5},{4,2},{5,3},{6,0},{7,1},{8,14},{9,15},{10,... | collective-permute-start | bytes 233480 | tf_op jit(solution)/shard_map/ppermute | solution.py:360
  8.2 0.8 %collective-permute-start.4 = (f32[5,152,128]{2,1,0:T(8,128)S(1)}, f32[5,152,128]{2,1,0:T(8,128)S(1)}, u32[]{:S(2)}, u32[]{:S(2)}) collective-permute-start(f32[5,152,128]{2,1,0:T(8,128)S(1)} %get-tuple-element.47), channel_id=1, source_target_pairs={{0,2},{1,3},{2,6},{3,7},{4,0},{5,1},{6,4},{7,5},{8,10},{9,11},{10,... | collective-permute-start | bytes 1167368 | tf_op jit(solution)/shard_map/ppermute | solution.py:360
  9.0 1.3 %copy-done = f32[1,64,4608]{2,1,0:T(8,128)S(1)} copy-done((f32[1,64,4608]{2,1,0:T(8,128)S(1)}, f32[1,64,4608]{2,1,0:T(8,128)}, u32[]{:S(2)}) %copy-start) | copy-done | bytes 1179672
  10.3 0.6 prepare_filters.1.refs_1_.refs_2_
  10.9 8.8 %collective-permute-done.1.refs_1_ = f32[1,152,128]{2,1,0:T(8,128)S(1)} collective-permute-done((f32[1,152,128]{2,1,0:T(8,128)S(1)}, f32[1,152,128]{2,1,0:T(8,128)S(1)}, u32[]{:S(2)}, u32[]{:S(2)}) %collective-permute-start.1) | collective-permute-done | bytes 77856 | tf_op jit(solution)/shard_map/ppermute | solution.py:360
  19.7 0.6 prepare_grad.2
  20.3 2.0 %multiply.5 = (f32[152,128]{1,0:T(8,128)S(1)}, f32[1152,512]{1,0:T(8,128)S(1)}) custom-call(f32[5,152,128]{2,1,0:T(8,128)S(1)} %get-tuple-element.43.refs_0_, bf16[1152,1536]{1,0:T(8,128)(2,1)S(1)} %prepare_filters.1.refs_1_.refs_2_, bf16[1152,512]{1,0:T(8,128)(2,1)S(1)} %get-tuple-element.42.refs_2_), custom_call_target="tpu_custom_call" | custom-call | tf_op jit(solution)/shard_map/multiply/pallas_call | solution.py:18
  22.3 2.9 %collective-permute-start.3 = (f32[4,152,128]{2,1,0:T(8,128)S(1)}, f32[4,152,128]{2,1,0:T(8,128)S(1)}, u32[]{:S(2)}, u32[]{:S(2)}) collective-permute-start(f32[4,152,128]{2,1,0:T(8,128)S(1)} %slice.27), channel_id=1, source_target_pairs={{0,4},{1,5},{2,0},{3,1},{4,6},{5,7},{6,2},{7,3},{8,12},{9,13},{10,... | collective-permute-start | bytes 933896 | tf_op jit(solution)/shard_map/ppermute | solution.py:360
  25.3 10.8 %collective-permute-done.4.refs_0_ = f32[5,152,128]{2,1,0:T(8,128)S(1)} collective-permute-done((f32[5,152,128]{2,1,0:T(8,128)S(1)}, f32[5,152,128]{2,1,0:T(8,128)S(1)}, u32[]{:S(2)}, u32[]{:S(2)}) %collective-permute-start.4) | collective-permute-done | bytes 389152 | tf_op jit(solution)/shard_map/ppermute | solution.py:360
  36.0 0.6 prepare_grad.3
  36.6 2.8 %multiply.6 = (f32[152,128]{1,0:T(8,128)S(1)}, f32[152,128]{1,0:T(8,128)S(1)}, f32[1152,512]{1,0:T(8,128)S(1)}) custom-call(f32[5,152,128]{2,1,0:T(8,128)S(1)} %collective-permute-done.4.refs_0_, f32[5,152,128]{2,1,0:T(8,128)S(1)} %collective-permute-done.2.refs_1_, bf16[1152,1536]{1,0:T(8,128)(2,1)S(1)} %prepare_filters.1.refs_1_.refs_2_, ...), custom_call_target="tpu_custom_call" | custom-call | tf_op jit(solution)/shard_map/multiply/pallas_call | solution.py:18
  39.4 0.5 multiply.7
  40.1 0.5 multiply.8
  40.6 0.5 collective-permute-start.5
  41.1 0.8 %collective-permute-done.6 = f32[4,64,512]{2,1,0:T(8,128)S(1)} collective-permute-done((f32[4,64,512]{2,1,0:T(8,128)S(1)}, f32[4,64,512]{2,1,0:T(8,128)S(1)}, u32[]{:S(2)}, u32[]{:S(2)}) %collective-permute-start.6) | collective-permute-done | bytes 524320 | tf_op jit(solution)/shard_map/ppermute | solution.py:363
  42.0 2.5 %collective-permute-start.7 = (f32[64,512]{1,0:T(8,128)S(1)}, f32[64,512]{1,0:T(8,128)S(1)}, u32[]{:S(2)}, u32[]{:S(2)}) collective-permute-start(f32[64,512]{1,0:T(8,128)S(1)} %get-tuple-element.79), channel_id=1, source_target_pairs={{0,24},{8,16},{16,8},{24,0},{1,25},{9,17},{17,9},{25,1},{2,26},{10... | collective-permute-start | bytes 393224 | tf_op jit(solution)/shard_map/ppermute | solution.py:367
  44.6 0.5 collective-permute-start.12
  45.1 0.5 collective-permute-start.11
  45.7 3.1 %collective-permute-done.7.refs_3_ = f32[64,512]{1,0:T(8,128)S(1)} collective-permute-done((f32[64,512]{1,0:T(8,128)S(1)}, f32[64,512]{1,0:T(8,128)S(1)}, u32[]{:S(2)}, u32[]{:S(2)}) %collective-permute-start.7) | collective-permute-done | bytes 131104 | tf_op jit(solution)/shard_map/ppermute | solution.py:367
  48.8 3.0 %collective-permute-start.15 = (f32[64,640]{1,0:T(8,128)S(1)}, f32[64,640]{1,0:T(8,128)S(1)}, u32[]{:S(2)}, u32[]{:S(2)}) collective-permute-start(f32[64,640]{1,0:T(8,128)S(1)} %get-tuple-element.71), channel_id=1, source_target_pairs={{0,24},{8,16},{16,8},{24,0},{1,25},{9,17},{17,9},{25,1},{2,26},{10... | collective-permute-start | bytes 491528 | tf_op jit(solution)/shard_map/ppermute | solution.py:367
  51.8 1.0 %collective-permute-start.14 = (f32[64,640]{1,0:T(8,128)S(1)}, f32[64,640]{1,0:T(8,128)S(1)}, u32[]{:S(2)}, u32[]{:S(2)}) collective-permute-start(f32[64,640]{1,0:T(8,128)S(1)} %get-tuple-element.70), channel_id=1, source_target_pairs={{0,16},{8,24},{16,0},{24,8},{1,17},{9,25},{17,1},{25,9},{2,18},{10... | collective-permute-start | bytes 491528 | tf_op jit(solution)/shard_map/ppermute | solution.py:367
  52.9 0.8 %collective-permute-start.13 = (f32[64,640]{1,0:T(8,128)S(1)}, f32[64,640]{1,0:T(8,128)S(1)}, u32[]{:S(2)}, u32[]{:S(2)}) collective-permute-start(f32[64,640]{1,0:T(8,128)S(1)} %get-tuple-element.69), channel_id=1, source_target_pairs={{0,8},{8,0},{16,24},{24,16},{1,9},{9,1},{17,25},{25,17},{2,10},{10... | collective-permute-start | bytes 491528 | tf_op jit(solution)/shard_map/ppermute | solution.py:367
  53.7 1.3 %multiply.9 = f32[152,128]{1,0:T(8,128)S(1)} custom-call(f32[4,152,128]{2,1,0:T(8,128)S(1)} %collective-permute-done.3.refs_0_, bf16[1152,1536]{1,0:T(8,128)(2,1)S(1)} %prepare_filters.1.refs_1_.refs_2_), custom_call_target="tpu_custom_call" | custom-call | tf_op jit(solution)/shard_map/multiply/pallas_call | solution.py:18
  55.0 2.5 %collective-permute-start.9 = (f32[152,128]{1,0:T(8,128)S(1)}, f32[152,128]{1,0:T(8,128)S(1)}, u32[]{:S(2)}, u32[]{:S(2)}) collective-permute-start(f32[152,128]{1,0:T(8,128)S(1)} %multiply.9), channel_id=1, source_target_pairs={{0,6},{1,7},{2,4},{3,5},{4,2},{5,3},{6,0},{7,1},{8,14},{9,15},{10,... | collective-permute-start | bytes 233480 | tf_op jit(solution)/shard_map/ppermute | solution.py:360
  57.5 4.4 %collective-permute-done.10.refs_3_ = f32[152,128]{1,0:T(8,128)S(1)} collective-permute-done((f32[152,128]{1,0:T(8,128)S(1)}, f32[152,128]{1,0:T(8,128)S(1)}, u32[]{:S(2)}, u32[]{:S(2)}) %collective-permute-start.10) | collective-permute-done | bytes 77856 | tf_op jit(solution)/shard_map/ppermute | solution.py:360
  62.0 4.4 %collective-permute-done.8.refs_1_ = f32[152,128]{1,0:T(8,128)S(1)} collective-permute-done((f32[152,128]{1,0:T(8,128)S(1)}, f32[152,128]{1,0:T(8,128)S(1)}, u32[]{:S(2)}, u32[]{:S(2)}) %collective-permute-start.8) | collective-permute-done | bytes 77856 | tf_op jit(solution)/shard_map/ppermute | solution.py:360
  66.4 0.8 %join_output.1 = f32[3,7,7,512]{3,2,1,0:T(8,128)} custom-call(f32[152,128]{1,0:T(8,128)S(1)} %get-tuple-element.62.refs_0_, f32[152,128]{1,0:T(8,128)S(1)} %collective-permute-done.8.refs_1_, f32[152,128]{1,0:T(8,128)S(1)} %collective-permute-done.9.refs_2_, f32[152,128]{1,0:T(8,128)S(1)} %collective-permute-done.10.refs_3_), custom_call_target="tpu_custom_call" | custom-call | tf_op jit(solution)/shard_map/join_output/pallas_call | solution.py:18
  67.2 0.8 %sum_replicas.1 = f32[1,64,1152]{2,1,0:T(8,128)} custom-call(f32[64,512]{1,0:T(8,128)S(1)} %get-tuple-element.68.refs_0_, f32[64,512]{1,0:T(8,128)S(1)} %collective-permute-done.11.refs_1_, f32[64,512]{1,0:T(8,128)S(1)} %collective-permute-done.12.refs_2_, f32[64,512]{1,0:T(8,128)S(1)} %collective-permute-done.7.refs_3_, ...), custom_call_target="tpu_custom_call" | custom-call | tf_op jit(solution)/shard_map/sum_replicas/pallas_call | solution.py:18
  (22 shorter events, 0.5 us)
Async XLA Ops:
  0.6 8.4 %collective-permute-start = (f32[1,64,4608]{2,1,0:T(8,128)}, f32[1,64,4608]{2,1,0:T(8,128)S(1)}, u32[]{:S(2)}, u32[]{:S(2)}) collective-permute-start(f32[1,64,4608]{2,1,0:T(8,128)} %own_ref), channel_id=1, source_target_pairs={{0,1},{1,0},{2,3},{3,2},{4,5},{5,4},{6,7},{7,6},{8,9},{9,8},{10,11... | collective-permute-start | bytes 3538952 | tf_op jit(solution)/shard_map/ppermute | solution.py:363
  1.1 1.0 %copy-start.1 = (f32[3,7,7,512]{3,2,1,0:T(8,128)S(1)}, f32[3,7,7,512]{3,2,1,0:T(8,128)}, u32[]{:S(2)}) copy-start(f32[3,7,7,512]{3,2,1,0:T(8,128)} %image_ref) | copy-start | bytes 903172
  2.1 1.0 %copy-start.2 = (f32[3,7,7,512]{3,2,1,0:T(8,128)S(1)}, f32[3,7,7,512]{3,2,1,0:T(8,128)}, u32[]{:S(2)}) copy-start(f32[3,7,7,512]{3,2,1,0:T(8,128)} %grad_ref.1) | copy-start | bytes 903172
  3.2 19.1 %collective-permute-start.2 = (f32[5,152,128]{2,1,0:T(8,128)S(1)}, f32[5,152,128]{2,1,0:T(8,128)S(1)}, u32[]{:S(2)}, u32[]{:S(2)}) collective-permute-start(f32[5,152,128]{2,1,0:T(8,128)S(1)} %get-tuple-element.43.refs_0_), channel_id=1, source_target_pairs={{0,4},{1,5},{2,0},{3,1},{4,6},{5,7},{6,2},{7,3},{8,12},{9,13},{10,... | collective-permute-start | bytes 1167368 | tf_op jit(solution)/shard_map/ppermute | solution.py:360
  6.9 12.9 %collective-permute-start.1 = (f32[1,152,128]{2,1,0:T(8,128)S(1)}, f32[1,152,128]{2,1,0:T(8,128)S(1)}, u32[]{:S(2)}, u32[]{:S(2)}) collective-permute-start(f32[1,152,128]{2,1,0:T(8,128)S(1)} %get-tuple-element.41), channel_id=1, source_target_pairs={{0,6},{1,7},{2,4},{3,5},{4,2},{5,3},{6,0},{7,1},{8,14},{9,15},{10,... | collective-permute-start | bytes 233480 | tf_op jit(solution)/shard_map/ppermute | solution.py:360
  8.2 27.8 %collective-permute-start.4 = (f32[5,152,128]{2,1,0:T(8,128)S(1)}, f32[5,152,128]{2,1,0:T(8,128)S(1)}, u32[]{:S(2)}, u32[]{:S(2)}) collective-permute-start(f32[5,152,128]{2,1,0:T(8,128)S(1)} %get-tuple-element.47), channel_id=1, source_target_pairs={{0,2},{1,3},{2,6},{3,7},{4,0},{5,1},{6,4},{7,5},{8,10},{9,11},{10,... | collective-permute-start | bytes 1167368 | tf_op jit(solution)/shard_map/ppermute | solution.py:360
  9.0 1.3 %copy-start = (f32[1,64,4608]{2,1,0:T(8,128)S(1)}, f32[1,64,4608]{2,1,0:T(8,128)}, u32[]{:S(2)}) copy-start(f32[1,64,4608]{2,1,0:T(8,128)} %own_ref) | copy-start | bytes 3538948
  22.3 17.1 %collective-permute-start.3 = (f32[4,152,128]{2,1,0:T(8,128)S(1)}, f32[4,152,128]{2,1,0:T(8,128)S(1)}, u32[]{:S(2)}, u32[]{:S(2)}) collective-permute-start(f32[4,152,128]{2,1,0:T(8,128)S(1)} %slice.27), channel_id=1, source_target_pairs={{0,4},{1,5},{2,0},{3,1},{4,6},{5,7},{6,2},{7,3},{8,12},{9,13},{10,... | collective-permute-start | bytes 933896 | tf_op jit(solution)/shard_map/ppermute | solution.py:360
  39.9 2.0 %collective-permute-start.6 = (f32[4,64,512]{2,1,0:T(8,128)S(1)}, f32[4,64,512]{2,1,0:T(8,128)S(1)}, u32[]{:S(2)}, u32[]{:S(2)}) collective-permute-start(f32[4,64,512]{2,1,0:T(8,128)S(1)} %get-tuple-element.63), channel_id=1, source_target_pairs={{0,1},{1,0},{2,3},{3,2},{4,5},{5,4},{6,7},{7,6},{8,9},{9,8},{10,11... | collective-permute-start | bytes 1572872 | tf_op jit(solution)/shard_map/ppermute | solution.py:363
  40.6 5.0 %collective-permute-start.5 = (f32[4,64,640]{2,1,0:T(8,128)S(1)}, f32[4,64,640]{2,1,0:T(8,128)S(1)}, u32[]{:S(2)}, u32[]{:S(2)}) collective-permute-start(f32[4,64,640]{2,1,0:T(8,128)S(1)} %get-tuple-element.60), channel_id=1, source_target_pairs={{0,1},{1,0},{2,3},{3,2},{4,5},{5,4},{6,7},{7,6},{8,9},{9,8},{10,11... | collective-permute-start | bytes 1966088 | tf_op jit(solution)/shard_map/ppermute | solution.py:363
  42.0 6.8 %collective-permute-start.7 = (f32[64,512]{1,0:T(8,128)S(1)}, f32[64,512]{1,0:T(8,128)S(1)}, u32[]{:S(2)}, u32[]{:S(2)}) collective-permute-start(f32[64,512]{1,0:T(8,128)S(1)} %get-tuple-element.79), channel_id=1, source_target_pairs={{0,24},{8,16},{16,8},{24,0},{1,25},{9,17},{17,9},{25,1},{2,26},{10... | collective-permute-start | bytes 393224 | tf_op jit(solution)/shard_map/ppermute | solution.py:367
  44.6 7.3 %collective-permute-start.12 = (f32[64,512]{1,0:T(8,128)S(1)}, f32[64,512]{1,0:T(8,128)S(1)}, u32[]{:S(2)}, u32[]{:S(2)}) collective-permute-start(f32[64,512]{1,0:T(8,128)S(1)} %get-tuple-element.76), channel_id=1, source_target_pairs={{0,16},{8,24},{16,0},{24,8},{1,17},{9,25},{17,1},{25,9},{2,18},{10... | collective-permute-start | bytes 393224 | tf_op jit(solution)/shard_map/ppermute | solution.py:367
  45.1 7.8 %collective-permute-start.11 = (f32[64,512]{1,0:T(8,128)S(1)}, f32[64,512]{1,0:T(8,128)S(1)}, u32[]{:S(2)}, u32[]{:S(2)}) collective-permute-start(f32[64,512]{1,0:T(8,128)S(1)} %get-tuple-element.77), channel_id=1, source_target_pairs={{0,8},{8,0},{16,24},{24,16},{1,9},{9,1},{17,25},{25,17},{2,10},{10... | collective-permute-start | bytes 393224 | tf_op jit(solution)/shard_map/ppermute | solution.py:367
  48.8 18.3 %collective-permute-start.15 = (f32[64,640]{1,0:T(8,128)S(1)}, f32[64,640]{1,0:T(8,128)S(1)}, u32[]{:S(2)}, u32[]{:S(2)}) collective-permute-start(f32[64,640]{1,0:T(8,128)S(1)} %get-tuple-element.71), channel_id=1, source_target_pairs={{0,24},{8,16},{16,8},{24,0},{1,25},{9,17},{17,9},{25,1},{2,26},{10... | collective-permute-start | bytes 491528 | tf_op jit(solution)/shard_map/ppermute | solution.py:367
  51.8 15.3 %collective-permute-start.14 = (f32[64,640]{1,0:T(8,128)S(1)}, f32[64,640]{1,0:T(8,128)S(1)}, u32[]{:S(2)}, u32[]{:S(2)}) collective-permute-start(f32[64,640]{1,0:T(8,128)S(1)} %get-tuple-element.70), channel_id=1, source_target_pairs={{0,16},{8,24},{16,0},{24,8},{1,17},{9,25},{17,1},{25,9},{2,18},{10... | collective-permute-start | bytes 491528 | tf_op jit(solution)/shard_map/ppermute | solution.py:367
  52.9 14.3 %collective-permute-start.13 = (f32[64,640]{1,0:T(8,128)S(1)}, f32[64,640]{1,0:T(8,128)S(1)}, u32[]{:S(2)}, u32[]{:S(2)}) collective-permute-start(f32[64,640]{1,0:T(8,128)S(1)} %get-tuple-element.69), channel_id=1, source_target_pairs={{0,8},{8,0},{16,24},{24,16},{1,9},{9,1},{17,25},{25,17},{2,10},{10... | collective-permute-start | bytes 491528 | tf_op jit(solution)/shard_map/ppermute | solution.py:367
  53.7 8.3 %collective-permute-start.10 = (f32[152,128]{1,0:T(8,128)S(1)}, f32[152,128]{1,0:T(8,128)S(1)}, u32[]{:S(2)}, u32[]{:S(2)}) collective-permute-start(f32[152,128]{1,0:T(8,128)S(1)} %get-tuple-element.67), channel_id=1, source_target_pairs={{0,2},{1,3},{2,6},{3,7},{4,0},{5,1},{6,4},{7,5},{8,10},{9,11},{10,... | collective-permute-start | bytes 233480 | tf_op jit(solution)/shard_map/ppermute | solution.py:360
  55.0 7.0 %collective-permute-start.9 = (f32[152,128]{1,0:T(8,128)S(1)}, f32[152,128]{1,0:T(8,128)S(1)}, u32[]{:S(2)}, u32[]{:S(2)}) collective-permute-start(f32[152,128]{1,0:T(8,128)S(1)} %multiply.9), channel_id=1, source_target_pairs={{0,6},{1,7},{2,4},{3,5},{4,2},{5,3},{6,0},{7,1},{8,14},{9,15},{10,... | collective-permute-start | bytes 233480 | tf_op jit(solution)/shard_map/ppermute | solution.py:360
  62.0 4.4 %collective-permute-start.8 = (f32[152,128]{1,0:T(8,128)S(1)}, f32[152,128]{1,0:T(8,128)S(1)}, u32[]{:S(2)}, u32[]{:S(2)}) collective-permute-start(f32[152,128]{1,0:T(8,128)S(1)} %get-tuple-element.64), channel_id=1, source_target_pairs={{0,4},{1,5},{2,0},{3,1},{4,6},{5,7},{6,2},{7,3},{8,12},{9,13},{10,... | collective-permute-start | bytes 233480 | tf_op jit(solution)/shard_map/ppermute | solution.py:360
